TPU v7x, 128 devices: a whole 4x4x4 slice. The times are simulated.
128 devices in a mesh: chan: 64 (over z, x, y_lo, core), win: 2 (over y_hi).
Axes of the slice: x: 4, y: 4 (y_hi: 2, y_lo: 2; y = y_hi * 2 + y_lo), z: 4, core: 2. Of those that a mesh axis runs over, the one named last changes fastest.
Arguments:
- series: bfloat16 [32, 3000, 8192], P('win', None, 'chan'), may hold values from -96 to 96
- block_ids: int32 [4], replicated, may hold values from 0 to 63
Outputs:
- stacked: bfloat16 [96, 512, 2, 8192], P('win', None, None, 'chan')
All inputs are finite; a program needn't handle non-finite values.
Results may differ from a plain program's by a relative error of at most 0.0056.
Values may be sent and summed in bfloat16 or wider, within the bound.
A program may use at most 192 MiB of HBM per device.

v0:
```python
import math

import jax
import jax.numpy as jnp
from jax import lax
from jax.sharding import PartitionSpec as P

F_LO = 6
NFREQ = 96
BLOCK = 128


def broadcast(value, axis, root):
    mine = lax.axis_index(axis) == root
    return lax.psum(jnp.where(mine, value, jnp.zeros_like(value)), axis)


def make_tables(length):
    positions = jnp.arange(length, dtype=jnp.int32)
    bins = F_LO + jnp.arange(NFREQ, dtype=jnp.int32)
    phases = bins[:, None] * positions[None, :] % length
    angles = 2.0 * math.pi / length * phases.astype(jnp.float32)
    table = jnp.concatenate([jnp.cos(angles), -jnp.sin(angles)], axis=0).astype(jnp.bfloat16)
    hann = 0.5 - 0.5 * jnp.cos(2.0 * math.pi / length * positions.astype(jnp.float32))
    return (table, hann)


def cross_spectra(sources, whitened):
    left = jnp.concatenate([sources[:, 0], sources[:, 1]], axis=0)
    right = jnp.stack(
        [
            jnp.concatenate([whitened[:, 0], whitened[:, 1]], axis=0),
            jnp.concatenate([whitened[:, 1], -whitened[:, 0]], axis=0),
        ],
        axis=2,
    )
    return jnp.einsum("wfs,wfpc->fspc", left, right, preferred_element_type=jnp.float32)


def local(series, block_ids):
    wins, length, chans = series.shape
    table, hann = make_tables(length)
    values = series.astype(jnp.float32)
    level = jnp.sqrt(jnp.mean(values * values, axis=1, keepdims=True) + 1e-06)
    clipped = jnp.clip(values, -2.0 * level, 2.0 * level)
    tapered = (clipped * hann[None, :, None]).astype(jnp.bfloat16)
    spectrum = jnp.einsum("kt,wtc->wkc", table, tapered, preferred_element_type=jnp.float32)
    power = jnp.sum(spectrum * spectrum, axis=1, keepdims=True) / NFREQ
    whitened = (
        (spectrum * lax.rsqrt(power + 1e-06)).astype(jnp.bfloat16).reshape(wins, 2, NFREQ, chans)
    )
    per_device = chans // BLOCK
    count_blocks = block_ids.shape[0]
    pieces = []
    for number in range(count_blocks):
        block = block_ids[number]
        owner = block // per_device
        pieces.append(broadcast(whitened, "chan", owner))
    sources = jnp.concatenate(pieces, axis=3)
    windows_total = wins * lax.axis_size("win")
    summed_stack = lax.psum_scatter(
        cross_spectra(sources, whitened), "win", scatter_dimension=0, tiled=True
    )
    return (summed_stack / windows_total).astype(jnp.bfloat16)


def solution(mesh):
    return jax.shard_map(
        local,
        mesh=mesh,
        in_specs=(P("win", None, "chan"), P()),
        out_specs=P("win", None, None, "chan"),
        check_vma=False,
    )
```

profile of v0, /device:TPU:1, one launch (start us, length us, event | category | flops | bytes accessed | tf_op | source)
XLA Modules:
  0.0 1199.2 jit_solution(9259185628572822834)
XLA Ops:
  6.5 0.0 all-reduce.3.cloned.1.call-start
  6.5 0.1 multiply_subtract_fusion
  6.6 1.5 fusion.25
  10.7 6.9 fusion
  17.6 5.4 cosine_convert_fusion
  22.9 7.8 multiply_reduce_fusion
  30.7 0.2 multiply_convert_fusion.1
  30.9 2.2 fusion.24
  33.1 0.0 all-reduce.3.cloned.1.call-update
  33.2 0.2 reduce-scatter.2.cloned.1.call-start
  33.4 0.1 fusion.23
  33.4 0.1 slice_bitcast_fusion.3
  33.6 1.4 maximum_bitcast_fusion.4
  35.0 558.3 %all-reduce.3.cloned.1.call-done = (bf16[16,2,96,128]{3,0,2,1:T(8,128)(2,1)}, bf16[16,2,96,128]{3,0,2,1:T(8,128)(2,1)}, bf16[16,2,96,128]{3,0,2,1:T(8,128)(2,1)}, bf16[16,2,96,128]{3,0,2,1:T(8,128)(2,1)}) async-done(((bf16[16,2,96,128]{3,0,2,1:T(8,128)(2,1)}, bf16[16,2,96,128]{3,0,2,1:T(8,128)(2,1)}, bf16[16,2,96,128]{3,0,2,1:T(8,128)(2,1)}, bf16[16,2,96,128]{3,0,2,1:T(8,128)(2,1)}), ...) | async-done | bytes 3145744 | tf_op jit(solution)/shard_map/psum | solution.py:15
  593.3 0.0 copy-start.1
  593.3 0.0 copy-start
  593.3 1.5 constant_dynamic-update-slice_fusion.3
  594.8 1.4 constant_dynamic-update-slice_fusion.2
  596.2 0.0 copy-done.1
  596.2 0.3 constant_dynamic-update-slice_fusion.1
  596.5 0.0 copy-done
  596.5 0.3 constant_dynamic-update-slice_fusion
  596.8 0.3 slice_bitcast_fusion.1
  597.1 20.7 %fusion.6 = f32[96,512,2,128]{3,1,2,0:T(8,128)} fusion(bf16[16,96,512]{2,0,1:T(8,128)(2,1)S(1)} %get-tuple-element.10, bf16[16,96,512]{2,0,1:T(8,128)(2,1)S(1)} %get-tuple-element.9, bf16[32,96,1,128]{3,0,2,1:T(8,128)(2,1)} %get-tuple-element.19, bf16[32,96,1,128]{3,0,2,1:T(8,128)(2,1)} %get-tuple-element.18), kind=kOutput, calls=%fused_computation.9 | convolution fusion | flops 814743552 | bytes 55050240 | tf_op jit(solution)/shard_map/wfs,wfpc->fspc/dot_general | solution.py:37
  617.8 0.0 reduce-scatter.2.cloned.1.call-update
  617.9 553.6 %reduce-scatter.2.cloned.1.call-done = f32[48,512,2,128]{3,1,2,0:T(8,128)} async-done(((f32[96,512,2,128]{3,1,2,0:T(8,128)}), f32[48,512,2,128]{3,1,2,0:T(8,128)}) %reduce-scatter.2.cloned.1.call-update) | async-done | bytes 25165840 | tf_op jit(solution)/shard_map/reduce_scatter | solution.py:61
  1171.5 9.7 multiply_convert_fusion
  1181.2 11.2 copy.10
  (3 shorter events, 0.0 us)
Async XLA Ops:
  6.5 586.8 %all-reduce.3.cloned.1.call-start = ((), (), s32[]{:S(2)}) async-start(), calls=%async_computation.2 | async-start | bytes 6291456 | tf_op jit(solution)/shard_map/psum | solution.py:15
  33.2 1138.3 %reduce-scatter.2.cloned.1.call-start = ((), (), s32[]{:S(2)}) async-start(), calls=%async_computation.1 | async-start | bytes 75497472 | tf_op jit(solution)/shard_map/reduce_scatter | solution.py:61
  593.3 2.9 copy-start.1
  593.3 3.2 copy-start
Sparse Core Ops, SparseCore 0:
  33.3 560.0 all-reduce.2
  618.0 553.4 reduce-scatter.1
where the time goes:
time: 1200 us
  waiting for transfers between devices  1110 us (92%)
  matrix products  28.5 us (2%)
  other arithmetic  25.9 us (2%)
  local copies, waits for them, and re-layouts  16.5 us (1%)
  between operations  16.1 us (1%)
    psum x1, waiting for transfers between devices, broadcast(): return lax.psum(jnp.where(mine, value, jnp.zeros_like(value)), axis)  558 us
    reduce_scatter x1, waiting for transfers between devices, local(): lax.psum_scatter(cross_spectra(sources, whitened), 'win', scatter_dimensi...  554 us
  transfers between devices with their start and end apart: 2, of which 2 were waited for; matrix products, arithmetic and copies ran while one was open for 0% of the time, Pallas kernels for 0%

commit v1 on v0

v1 whole, which is shorter than its diff:
```python
import functools
import math

import jax
import jax.numpy as jnp
import numpy as np
from jax import lax
from jax.experimental import pallas as pl
from jax.experimental.pallas import tpu as pltpu
from jax.sharding import PartitionSpec as P

LENGTH = 3000
F_LO = 6
NFREQ = 96
WINDOWS = 32
HALF = NFREQ // 2
WINS = WINDOWS // 2
UNITS = 2 * HALF
MESH = pl.DeviceIdType.MESH
COL = (((0,), (0,)), ((), ()))


def make_table():
    positions = np.arange(LENGTH)
    bins = F_LO + np.arange(NFREQ)
    angles = 2.0 * math.pi / LENGTH * (bins[:, None] * positions[None, :] % LENGTH)
    hann = 0.5 - 0.5 * np.cos(2.0 * math.pi / LENGTH * positions)
    rows = np.stack([np.cos(angles), -np.sin(angles)], axis=1).reshape(2 * NFREQ, LENGTH)
    return jnp.asarray(rows * hann[None, :], jnp.bfloat16)


def spectra_kernel(table_ref, series_ref, out_ref, rows_ref):
    step = pl.program_id(0)
    clipped = []
    for k in range(2):
        values = series_ref[k].astype(jnp.float32)
        level = 2.0 * jnp.sqrt(jnp.mean(values * values, axis=0, keepdims=True) + 1e-6)
        clipped.append(jnp.clip(values, -level, level).astype(jnp.bfloat16))
    spectrum = jnp.dot(
        table_ref[...], jnp.concatenate(clipped, axis=1), preferred_element_type=jnp.float32
    )
    power = jnp.sum(spectrum * spectrum, axis=0, keepdims=True) / NFREQ
    whitened = spectrum * lax.rsqrt(power + 1e-6)
    for k in range(2):
        rows_ref[pl.ds(2 * step + k, 2 * NFREQ, WINS), :] = whitened[:, 128 * k : 128 * (k + 1)]

    @pl.when(step == WINS // 2 - 1)
    def _():
        out_ref[...] = rows_ref[...].reshape(2 * NFREQ, WINS, 128).astype(jnp.bfloat16)


def spectra(series):
    return pl.pallas_call(
        spectra_kernel,
        grid=(WINS // 2,),
        in_specs=[
            pl.BlockSpec((2 * NFREQ, LENGTH), lambda i: (0, 0)),
            pl.BlockSpec((2, LENGTH, 128), lambda i: (i, 0, 0)),
        ],
        out_specs=pl.BlockSpec((2 * NFREQ, WINS, 128), lambda i: (0, 0, 0)),
        out_shape=jax.ShapeDtypeStruct((2 * NFREQ, WINS, 128), jnp.bfloat16),
        scratch_shapes=[pltpu.VMEM((2 * NFREQ * WINS, 128), jnp.float32)],
        compiler_params=pltpu.CompilerParams(vmem_limit_bytes=58 * 2**20),
    )(make_table(), series)


def exchange_kernel(
    ids_ref, v_ref, src_ref, rhs_ref, p1, q1, p2, q2, p3, q3,
    win_sem, a1_send, a1_recv, a2_send, a2_recv, y_send, y_recv,
    b1_send, b1_recv, b2_send, b2_recv, c_send, c_recv, l_sem,
):
    me = lax.axis_index("chan")
    w = lax.axis_index("win")
    z, x, y, c = me // 16, me // 4 % 4, me // 2 % 2, me % 2

    def chan(z, x, y, c):
        return ((z * 4 + x) * 2 + y) * 2 + c

    def plane(h, a, b, c):
        return chan(jnp.where(h == 0, a, b), jnp.where(h == 0, b, a), y, c)

    ring = [(k, m) for k in range(4) for m in range(2) if (k, m) != (0, 0)]
    column = [(1, 0), (0, 1), (1, 1)]
    coords = (z, x)

    barrier = pltpu.get_barrier_semaphore()
    peers = [(plane(0, (z + k) % 4, x, (c + m) % 2), w) for k, m in ring]
    peers += [(plane(1, (x + k) % 4, z, (c + m) % 2), w) for k, m in ring if k]
    peers += [(chan(z, x, (y + dy) % 2, c), (w + dw) % 2) for dy, dw in column]
    for peer in peers:
        pl.semaphore_signal(barrier, inc=1, device_id=peer, device_id_type=MESH)
    pl.semaphore_wait(barrier, len(peers))

    def remote(src, dst, send, recv, peer):
        copy = pltpu.make_async_remote_copy(
            src_ref=src, dst_ref=dst, send_sem=send, recv_sem=recv,
            device_id=peer, device_id_type=MESH,
        )
        copy.start()
        return copy

    first = []
    for k, m in ring:
        for h in range(2):
            a, b = coords[h], coords[1 - h]
            to_a, to_c = (a + k) % 4, (c + m) % 2
            slot = k * 2 + m
            first.append(
                remote(
                    v_ref.at[pl.ds(h * UNITS + (to_a * 2 + to_c) * 12, 12)],
                    p1.at[h, a * 2 + c],
                    a1_send.at[h, slot], a1_recv.at[h, slot],
                    (plane(h, to_a, b, to_c), w),
                )
            )
    window = remote(
        v_ref.at[pl.ds((1 - w) * UNITS, UNITS)], rhs_ref.at[w],
        win_sem.at[0], win_sem.at[1], (me, 1 - w),
    )
    own_rhs = pltpu.make_async_copy(v_ref.at[pl.ds(w * UNITS, UNITS)], rhs_ref.at[w], l_sem.at[0])
    own_rhs.start()
    for h in range(2):
        a = coords[h]
        p1[h, a * 2 + c] = v_ref[pl.ds(h * UNITS + (a * 2 + c) * 12, 12)]
    for copy in first:
        copy.wait()

    where = []
    for j in range(4):
        block = ids_ref[j]
        where.append((block // 16, block // 4 % 4, block // 2 % 2, block % 2))

    second = []
    for h in range(2):
        a, b = coords[h], coords[1 - h]
        for j in range(4):
            own = where[j]
            q1[h, j] = p1[h, own[h] * 2 + own[3]]
        for k in range(1, 4):
            to_b = (b + k) % 4
            second.append(
                remote(
                    q1.at[h, :, pl.ds(to_b * 3, 3)], p2.at[h, b],
                    a2_send.at[h, k], a2_recv.at[h, k],
                    (plane(h, a, to_b, c), w),
                )
            )
        p2[h, b] = q1[h, :, pl.ds(b * 3, 3)]
    for copy in second:
        copy.wait()

    third = []
    for h in range(2):
        for j in range(4):
            q2[h, j] = p2[h, where[j][1 - h], j]
    for n, (dy, dw) in enumerate(column):
        to_y, to_w = (y + dy) % 2, (w + dw) % 2
        third.append(
            remote(
                q2.at[to_w], p3.at[w, y], y_send.at[n], y_recv.at[n],
                (chan(z, x, to_y, c), to_w),
            )
        )
    p3[w, y] = q2[w]
    for copy in third:
        copy.wait()
    for j in range(4):
        for g in range(2):
            q3[j, g] = p3[g, where[j][2], j]

    a = jnp.where(w == 0, z, x)
    b = jnp.where(w == 0, x, z)
    keep = pltpu.make_async_copy(q3, src_ref.at[:, :, a, c, b], l_sem.at[1])
    keep.start()
    pairs = (pl.ds(0, 2), pl.ds(2, 2))
    fourth = []
    for k in range(1, 4):
        for g in range(2):
            to = ((a + k) % 4, b) if g == 0 else (a, (b + k) % 4)
            fourth.append(
                remote(
                    q3.at[pairs[g]], src_ref.at[pairs[g], :, a, c, b],
                    b1_send.at[g, k], b1_recv.at[g, k],
                    (plane(w, to[0], to[1], c), w),
                )
            )
    keep.wait()
    for copy in fourth:
        copy.wait()

    def line(g, a, b):
        if g == 0:
            return src_ref.at[pairs[0], :, :, c, b]
        return src_ref.at[pairs[1], :, a, c, :]

    fifth = []
    for k in range(1, 4):
        for g in range(2):
            to = (a, (b + k) % 4) if g == 0 else ((a + k) % 4, b)
            fifth.append(
                remote(
                    line(g, a, b), line(g, a, b), b2_send.at[g, k], b2_recv.at[g, k],
                    (plane(w, to[0], to[1], c), w),
                )
            )
    sibling = (chan(z, x, y, 1 - c), w)
    last = []
    for g in range(2):
        last.append(
            remote(line(g, a, b), line(g, a, b), c_send.at[g, 0], c_recv.at[g, 0], sibling)
        )
    number = 0
    for k in range(1, 4):
        for g in range(2):
            fifth[number].wait()
            number += 1
            ref = line(g, (a - k + 4) % 4, (b - k + 4) % 4)
            last.append(remote(ref, ref, c_send.at[g, k], c_recv.at[g, k], sibling))
    for copy in last:
        copy.wait()
    window.wait()
    own_rhs.wait()


def exchange(block_ids, white):
    dma = pltpu.SemaphoreType.DMA
    vmem = lambda *shape: pltpu.VMEM(shape + (WINS, 128), jnp.bfloat16)
    return pl.pallas_call(
        exchange_kernel,
        out_shape=[
            jax.ShapeDtypeStruct((4, 2, 4, 2, 4, 3, WINS, 128), jnp.bfloat16),
            jax.ShapeDtypeStruct((2, UNITS, WINS, 128), jnp.bfloat16),
        ],
        in_specs=[
            pl.BlockSpec(memory_space=pltpu.SMEM),
            pl.BlockSpec(memory_space=pltpu.VMEM),
        ],
        out_specs=[pl.BlockSpec(memory_space=pl.ANY), pl.BlockSpec(memory_space=pl.ANY)],
        scratch_shapes=[
            vmem(2, 8, 12), vmem(2, 4, 12), vmem(2, 4, 4, 3), vmem(2, 4, 3),
            vmem(2, 2, 4, 3), vmem(4, 2, 3),
            dma((2,)), dma((2, 8)), dma((2, 8)), dma((2, 4)), dma((2, 4)), dma((3,)), dma((3,)),
            dma((2, 4)), dma((2, 4)), dma((2, 4)), dma((2, 4)), dma((2, 4)), dma((2, 4)), dma((2,)),
        ],
        compiler_params=pltpu.CompilerParams(
            collective_id=0, has_side_effects=True, vmem_limit_bytes=40 * 2**20
        ),
    )(block_ids, white)


def stack_kernel(count, src_ref, rhs_ref, out_ref, rows_ref):
    for i in range(count):
        left = jnp.concatenate(
            [src_ref[j, :, 2 * i : 2 * i + 2].reshape(4 * WINS, 128) for j in range(4)], axis=1
        )
        real = [rhs_ref[g, 2 * i] * (1.0 / WINDOWS) for g in range(2)]
        imag = [rhs_ref[g, 2 * i + 1] * (1.0 / WINDOWS) for g in range(2)]
        right = jnp.concatenate(
            [
                jnp.concatenate([real[0], imag[0], real[1], imag[1]], axis=0),
                jnp.concatenate([imag[0], -real[0], imag[1], -real[1]], axis=0),
            ],
            axis=1,
        )
        total = lax.dot_general(left, right, COL, preferred_element_type=jnp.float32)
        rows_ref[i % 2, pl.ds(0, 512, 2), :] = total[:, :128]
        rows_ref[i % 2, pl.ds(1, 512, 2), :] = total[:, 128:]
        out_ref[i] = rows_ref[i % 2].astype(jnp.bfloat16)


def stack(sources, rhs):
    count = 8
    out = pl.pallas_call(
        functools.partial(stack_kernel, count),
        grid=(HALF // count,),
        in_specs=[
            pl.BlockSpec((4, 2, 2 * count, WINS, 128), lambda i: (0, 0, i, 0, 0)),
            pl.BlockSpec((2, 2 * count, WINS, 128), lambda i: (0, i, 0, 0)),
        ],
        out_specs=pl.BlockSpec((count, 1024, 128), lambda i: (i, 0, 0)),
        out_shape=jax.ShapeDtypeStruct((HALF, 1024, 128), jnp.bfloat16),
        scratch_shapes=[pltpu.VMEM((2, 1024, 128), jnp.float32)],
        compiler_params=pltpu.CompilerParams(vmem_limit_bytes=40 * 2**20),
    )(sources.reshape(4, 2, UNITS, WINS, 128), rhs)
    return out.reshape(HALF, 512, 2, 128)


def local(series, block_ids):
    sources, rhs = exchange(block_ids, spectra(series))
    return stack(sources, rhs)


def solution(mesh):
    return jax.shard_map(
        local,
        mesh=mesh,
        in_specs=(P("win", None, "chan"), P()),
        out_specs=P("win", None, None, "chan"),
        check_vma=False,
    )
```

time: 1200 us -> 64.3 us (0.05)
  waiting for transfers between devices: 1110 us -> 0 us
  Pallas kernels: 0 us -> 62.8 us
  matrix products: 28.5 us -> 0 us
  other arithmetic: 25.9 us -> 0 us
  between operations: 16.1 us -> 0.01 us
  local copies, waits for them, and re-layouts: 16.5 us -> 1.14 us
    psum x1 -> x0, waiting for transfers between devices: 558 us -> none  [broadcast(): return lax.psum(jnp.where(mine, value, jnp.zeros_like(value)), axis)]
    reduce_scatter x1 -> x0, waiting for transfers between devices: 554 us -> none  [local(): lax.psum_scatter(cross_spectra(sources, whitened), 'win', scatter_dimensi...]
    pallas_call x0 -> x3, Pallas kernels: none -> 62.8 us  [the longest x1 42.2 us: exchange(): pl.pallas_call(exchange_kernel, out_shape=[jax.ShapeDtypeStruct((4, 2, 4,...]
    dot_general x2 -> x0, matrix products: 28.5 us -> none  [the longest x1 20.7 us: cross_spectra(): jnp.einsum('wfs,wfpc->fspc', left, right, preferred_element_type=jnp.floa...]
  transfers between devices with their start and end apart: 2 -> 0, of which waited for: 2 -> 0; matrix products, arithmetic and copies ran while one was open for 0% -> 0% of each run, Pallas kernels for 0% -> 0%
where the time goes in v1:
time: 64.3 us; the launch traced here: 64 us
  Pallas kernels  62.8 us (98%)
  local copies, waits for them, and re-layouts  1.14 us (2%)
    pallas_call x1, Pallas kernels, exchange(): pl.pallas_call(exchange_kernel, out_shape=[jax.ShapeDtypeStruct((4, 2, 4,...  42.2 us
    pallas_call x1, Pallas kernels, spectra(): pl.pallas_call(spectra_kernel, grid=(WINS // 2,), in_specs=[pl.BlockSpec(...  12.7 us
    pallas_call x1, Pallas kernels, stack(): pl.pallas_call(functools.partial(stack_kernel, count), grid=(HALF // coun...  7.98 us

profile of v1, /device:TPU:1, one launch (start us, length us, event | category | flops | bytes accessed | tf_op | source)
XLA Modules:
  0.0 64.0 jit_solution(8865111116432335584)
XLA Ops:
  0.0 0.0 copy-start.1
  0.0 12.7 %shard_map.37.v_ref = bf16[192,16,128]{2,1,0:T(8,128)(2,1)} custom-call(bf16[192,3000]{1,0:T(8,128)(2,1)} %constant.2.clone.table_ref, bf16[16,3000,128]{2,1,0:T(8,128)(2,1)} %series_ref.1), custom_call_target="tpu_custom_call" | custom-call | tf_op jit(solution)/shard_map/pallas_call | solution.py:53
  12.7 0.0 copy-done.1
  12.7 0.0 copy-start
  12.7 1.1 %copy-done = bf16[192,16,128]{2,1,0:T(8,128)(2,1)S(1)} copy-done((bf16[192,16,128]{2,1,0:T(8,128)(2,1)S(1)}, bf16[192,16,128]{2,1,0:T(8,128)(2,1)}, u32[]{:S(2)}) %copy-start) | copy-done | bytes 786456
  13.8 42.2 %shard_map.38 = (bf16[4,2,4,2,4,3,16,128]{7,6,5,4,3,2,1,0:T(8,128)(2,1)S(1)}, bf16[2,96,16,128]{3,2,1,0:T(8,128)(2,1)S(1)}) custom-call(s32[4]{0:T(128)S(1)} %copy-done.1, bf16[192,16,128]{2,1,0:T(8,128)(2,1)S(1)} %copy-done), custom_call_target="tpu_custom_call" | custom-call | tf_op jit(solution)/shard_map/pallas_call | solution.py:228
  56.0 8.0 %shard_map.39 = bf16[48,1024,128]{2,1,0:T(8,128)(2,1)} custom-call(bf16[4,2,96,16,128]{4,3,2,1,0:T(8,128)(2,1)S(1)} %bitcast.2, bf16[2,96,16,128]{3,2,1,0:T(8,128)(2,1)S(1)} %get-tuple-element.8.rhs_ref), custom_call_target="tpu_custom_call" | custom-call | tf_op jit(solution)/shard_map/pallas_call | solution.py:273
Async XLA Ops:
  0.0 12.7 %copy-start.1 = (s32[4]{0:T(128)S(1)}, s32[4]{0:T(128)}, u32[]{:S(2)}) copy-start(s32[4]{0:T(128)} %ids_ref.1) | copy-start | bytes 52
  12.7 1.1 %copy-start = (bf16[192,16,128]{2,1,0:T(8,128)(2,1)S(1)}, bf16[192,16,128]{2,1,0:T(8,128)(2,1)}, u32[]{:S(2)}) copy-start(bf16[192,16,128]{2,1,0:T(8,128)(2,1)} %shard_map.37.v_ref) | copy-start | bytes 2359300

commit v2 on v1

v2 whole, which is shorter than its diff:
```python
import functools
import math

import jax
import jax.numpy as jnp
import numpy as np
from jax import lax
from jax.experimental import pallas as pl
from jax.experimental.pallas import tpu as pltpu
from jax.sharding import PartitionSpec as P

LENGTH = 3000
F_LO = 6
NFREQ = 96
WINDOWS = 32
HALF = NFREQ // 2
WINS = WINDOWS // 2
PART = WINS // 2
GROUP = 4
MESH = pl.DeviceIdType.MESH
COL = (((0,), (0,)), ((), ()))


def make_table():
    positions = np.arange(LENGTH)
    bins = F_LO + np.arange(NFREQ)
    angles = 2.0 * math.pi / LENGTH * (bins[:, None] * positions[None, :] % LENGTH)
    hann = 0.5 - 0.5 * np.cos(2.0 * math.pi / LENGTH * positions)
    rows = np.stack([np.cos(angles), -np.sin(angles)], axis=1).reshape(2 * NFREQ, LENGTH)
    return jnp.asarray(rows * hann[None, :], jnp.bfloat16)


def exchange_kernel(
    ids_ref, table_ref, series_ref, src_ref, rhs_ref,
    held, rows, v, p1_0, p1_1, q1, p2_0, p2_1, q2, p3, q3,
    s_sem, l_sem, w_send, w_recv, a1_send, a1_recv, a2_send, a2_recv, y_send, y_recv,
    b1_send, b1_recv, b2_send, b2_recv, c_send, c_recv,
):
    me = lax.axis_index("chan")
    w = lax.axis_index("win")
    z, x, y, c = me // 16, me // 4 % 4, me // 2 % 2, me % 2

    def chan(z, x, y, c):
        return ((z * 4 + x) * 2 + y) * 2 + c

    def plane(h, a, b, c):
        return chan(jnp.where(h == 0, a, b), jnp.where(h == 0, b, a), y, c)

    p1 = (p1_0, p1_1)
    p2 = (p2_0, p2_1)
    column = [(1, 0), (0, 1), (1, 1)]
    coords = (z, x)
    loads = []
    for n in range(WINS // GROUP):
        window = pl.ds(n * GROUP, GROUP)
        loads.append(pltpu.make_async_copy(series_ref.at[window], held.at[window], s_sem.at[n]))
        loads[-1].start()

    barrier = pltpu.get_barrier_semaphore()
    peers = [(plane(h, (coords[h] + k) % 4, coords[1 - h], (c + m) % 2), w)
             for h in range(2) for k in range(1, 4) for m in range(2)]
    peers += [(chan(z, x, y, 1 - c), w)]
    peers += [(chan(z, x, (y + dy) % 2, c), (w + dw) % 2) for dy, dw in column]
    for peer in peers:
        pl.semaphore_signal(barrier, inc=1, device_id=peer, device_id_type=MESH)

    def remote(src, dst, send, recv, peer):
        return pltpu.make_async_remote_copy(
            src_ref=src, dst_ref=dst, send_sem=send, recv_sem=recv,
            device_id=peer, device_id_type=MESH,
        )

    def transform(part, n):
        first = part * PART + n * GROUP
        clipped = []
        for k in range(GROUP):
            values = held[first + k].astype(jnp.float32)
            level = 2.0 * jnp.sqrt(jnp.mean(values * values, axis=0, keepdims=True) + 1e-6)
            clipped.append(jnp.clip(values, -level, level).astype(jnp.bfloat16))
        spectrum = jnp.dot(
            table_ref[...], jnp.concatenate(clipped, axis=1), preferred_element_type=jnp.float32
        )
        power = jnp.sum(spectrum * spectrum, axis=0, keepdims=True) / NFREQ
        whitened = spectrum * lax.rsqrt(power + 1e-6)
        for k in range(GROUP):
            rows[pl.ds(n * GROUP + k, 2 * NFREQ, PART), :] = whitened[:, 128 * k : 128 * (k + 1)]

    first = []
    windows = []
    for part in range(2):
        for n in range(PART // GROUP):
            loads[part * (PART // GROUP) + n].wait()
            transform(part, n)
        v[part] = rows[...].reshape(NFREQ, 2 * PART, 128).astype(jnp.bfloat16)
        if part == 0:
            pl.semaphore_wait(barrier, len(peers))
        other = (c + part) % 2
        for k in (1, 3, 2, 0):
            for h in range(2):
                a, b = coords[h], coords[1 - h]
                to_a = (a + k) % 4
                copy = remote(
                    v.at[part, pl.ds(h * HALF + to_a * 12, 12)], p1[h].at[a, c],
                    a1_send.at[part, h, k], a1_recv.at[h, k, other],
                    (plane(h, to_a, b, part if k else 1 - c), w),
                )
                if k:
                    copy.start()
                    first.append(copy)
                else:
                    pl.when(other == 1)(copy.start)
        windows.append(
            remote(
                v.at[part, pl.ds((1 - w) * HALF, HALF)], rhs_ref.at[w, part],
                w_send.at[part], w_recv.at[part], (me, 1 - w),
            )
        )
        windows[-1].start()
    own_rhs = pltpu.make_async_copy(v.at[:, pl.ds(w * HALF, HALF)], rhs_ref.at[w], l_sem.at[0])
    own_rhs.start()

    where = []
    for j in range(4):
        block = ids_ref[j]
        where.append((block // 16, block // 4 % 4, block // 2 % 2, block % 2))

    second = []
    for h in range(2):
        a, b = coords[h], coords[1 - h]
        p1[h][a, c] = v[c, pl.ds(h * HALF + a * 12, 12)]
        for k in range(4):
            for m in range(2):
                if k or m:
                    remote(
                        v.at[0, pl.ds(0, 12)], p1[h].at[a, c],
                        a1_send.at[0, h, k], a1_recv.at[h, k, m], (me, 1 - w),
                    ).wait_recv()
        for j in range(4):
            q1[h, j] = p1[h][where[j][h], where[j][3]]
        for k in (1, 3, 2):
            to_b = (b + k) % 4
            copy = remote(
                q1.at[h, :, pl.ds(to_b * 3, 3)], p2[h].at[b],
                a2_send.at[h, k], a2_recv.at[h, k], (plane(h, a, to_b, c), w),
            )
            copy.start()
            second.append(copy)
        p2[h][b] = q1[h, :, pl.ds(b * 3, 3)]

    for h in range(2):
        for copy in second[3 * h : 3 * h + 3]:
            copy.wait()
        for j in range(4):
            q2[h, j] = p2[h][where[j][1 - h], j]
    third = []
    for n, (dy, dw) in enumerate(column):
        to_y, to_w = (y + dy) % 2, (w + dw) % 2
        third.append(
            remote(
                q2.at[to_w], p3.at[w, y], y_send.at[n], y_recv.at[n],
                (chan(z, x, to_y, c), to_w),
            )
        )
        third[-1].start()
    p3[w, y] = q2[w]
    for copy in third:
        copy.wait()
    for j in range(4):
        for g in range(2):
            q3[j, g] = p3[g, where[j][2], j]

    a = jnp.where(w == 0, z, x)
    b = jnp.where(w == 0, x, z)
    slots = (pl.ds(0, 2), pl.ds(2, 2))

    def at(s, k, m):
        k, m = (4 - k) % 4, (4 - m) % 4
        return ((a + k) % 4, (b + m) % 4) if s == 0 else ((a + m) % 4, (b + k) % 4)

    def piece(s, k, m):
        pa, pb = at(s, k, m)
        return src_ref.at[slots[s], :, c, pa, pb]

    def line(s, m):
        pa, pb = at(s, 0, m)
        if s == 0:
            return src_ref.at[slots[s], :, c, :, pb]
        return src_ref.at[slots[s], :, c, pa]

    keep = pltpu.make_async_copy(q3, src_ref.at[:, :, c, a, b], l_sem.at[1])
    keep.start()
    fourth, fifth, last = {}, {}, []
    for k in (1, 3, 2):
        for s in range(2):
            to = at(s, 4 - k, 0)
            fourth[s, k] = remote(
                q3.at[slots[s]], piece(s, 0, 0), b1_send.at[s, k], b1_recv.at[s, k],
                (plane(w, to[0], to[1], c), w),
            )
            fourth[s, k].start()

    def forward(s, k):
        for m in (1, 3, 2):
            to = at(s, 0, 4 - m)
            fifth[s, k, m] = remote(
                q3.at[slots[s]] if k == 0 else piece(s, k, 0), piece(s, k, 0),
                b2_send.at[s, k, m], b2_recv.at[s, k, m], (plane(w, to[0], to[1], c), w),
            )
            fifth[s, k, m].start()

    for s in range(2):
        forward(s, 0)
    keep.wait()
    for k in (1, 3, 2):
        for s in range(2):
            fourth[s, k].wait()
            forward(s, k)
    sibling = (chan(z, x, y, 1 - c), w)
    for m in (0, 1, 3, 2):
        for s in range(2):
            if m:
                for k in range(4):
                    fifth[s, k, m].wait()
            last.append(remote(line(s, m), line(s, m), c_send.at[s, m], c_recv.at[s, m], sibling))
            last[-1].start()
    for copy in last:
        copy.wait()
    for copy in windows:
        copy.wait()
    own_rhs.wait()
    for copy in first:
        copy.wait_send()
    for h in range(2):
        remote(
            v.at[0, pl.ds(0, 12)], p1[h].at[0, 0], a1_send.at[1 - c, h, 0], a1_recv.at[h, 0, 1],
            sibling,
        ).wait_send()


def exchange(block_ids, series):
    dma = pltpu.SemaphoreType.DMA
    vmem = lambda *shape: pltpu.VMEM(shape + (2 * PART, 128), jnp.bfloat16)
    return pl.pallas_call(
        exchange_kernel,
        out_shape=[
            jax.ShapeDtypeStruct((4, 2, 2, 4, 4, 3, 2 * PART, 128), jnp.bfloat16),
            jax.ShapeDtypeStruct((2, 2, HALF, 2 * PART, 128), jnp.bfloat16),
        ],
        in_specs=[
            pl.BlockSpec(memory_space=pltpu.SMEM),
            pl.BlockSpec(memory_space=pltpu.VMEM),
            pl.BlockSpec(memory_space=pl.ANY),
        ],
        out_specs=[pl.BlockSpec(memory_space=pl.ANY), pl.BlockSpec(memory_space=pl.ANY)],
        scratch_shapes=[
            pltpu.VMEM((WINS, LENGTH, 128), jnp.bfloat16),
            pltpu.VMEM((2 * NFREQ * PART, 128), jnp.float32),
            vmem(2, NFREQ), vmem(4, 2, 12), vmem(4, 2, 12), vmem(2, 4, 12), vmem(4, 4, 3), vmem(4, 4, 3),
            vmem(2, 4, 3),
            vmem(2, 2, 4, 3), vmem(4, 2, 3),
            dma((WINS // GROUP,)), dma((2,)), dma((2,)), dma((2,)),
            dma((2, 2, 4)), dma((2, 4, 2)), dma((2, 4)), dma((2, 4)), dma((3,)), dma((3,)),
            dma((2, 4)), dma((2, 4)), dma((2, 4, 4)), dma((2, 4, 4)), dma((2, 4)), dma((2, 4)),
        ],
        compiler_params=pltpu.CompilerParams(
            collective_id=0, has_side_effects=True, vmem_limit_bytes=46 * 2**20
        ),
    )(block_ids, make_table(), series)


def stack_kernel(count, src_ref, rhs_ref, out_ref, rows_ref):
    for i in range(count):
        left = jnp.concatenate(
            [src_ref[j, :, :, i].reshape(8 * PART, 128) for j in range(4)], axis=1
        )
        tiles = [rhs_ref[g, part, i].astype(jnp.float32) * (1.0 / WINDOWS)
                 for g in range(2) for part in range(2)]
        turned = [t for tile in tiles for t in (tile[PART:], -tile[:PART])]
        right = jnp.concatenate(
            [jnp.concatenate(tiles, axis=0), jnp.concatenate(turned, axis=0)], axis=1
        ).astype(jnp.bfloat16)
        total = lax.dot_general(left, right, COL, preferred_element_type=jnp.float32)
        rows_ref[i % 2, pl.ds(0, 512, 2), :] = total[:, :128]
        rows_ref[i % 2, pl.ds(1, 512, 2), :] = total[:, 128:]
        out_ref[i] = rows_ref[i % 2].astype(jnp.bfloat16)


def stack(sources, rhs):
    count = 8
    out = pl.pallas_call(
        functools.partial(stack_kernel, count),
        grid=(HALF // count,),
        in_specs=[
            pl.BlockSpec((4, 2, 2, count, 2 * PART, 128), lambda i: (0, 0, 0, i, 0, 0)),
            pl.BlockSpec((2, 2, count, 2 * PART, 128), lambda i: (0, 0, i, 0, 0)),
        ],
        out_specs=pl.BlockSpec((count, 1024, 128), lambda i: (i, 0, 0)),
        out_shape=jax.ShapeDtypeStruct((HALF, 1024, 128), jnp.bfloat16),
        scratch_shapes=[pltpu.VMEM((2, 1024, 128), jnp.float32)],
        compiler_params=pltpu.CompilerParams(vmem_limit_bytes=40 * 2**20),
    )(sources.reshape(4, 2, 2, HALF, 2 * PART, 128), rhs)
    return out.reshape(HALF, 512, 2, 128)


def local(series, block_ids):
    sources, rhs = exchange(block_ids, series)
    return stack(sources, rhs)


def solution(mesh):
    return jax.shard_map(
        local,
        mesh=mesh,
        in_specs=(P("win", None, "chan"), P()),
        out_specs=P("win", None, None, "chan"),
        check_vma=False,
    )
```

time: 64.3 us -> 53.8 us (0.84)
  Pallas kernels: 62.8 us -> 51.7 us
  local copies, waits for them, and re-layouts: 1.14 us -> 1.92 us
    pallas_call x2 -> x1, Pallas kernels: 54.8 us -> 43.7 us  [exchange(): pl.pallas_call(exchange_kernel, out_shape=[jax.ShapeDtypeStruct((4, 2, 2,...]
    unnamed x4, local copies, waits for them, and re-layouts: 1.14 us -> 1.92 us
where the time goes in v2:
time: 53.8 us; the launch traced here: 53.6 us
  Pallas kernels  51.7 us (96%)
  local copies, waits for them, and re-layouts  1.92 us (4%)
    pallas_call x1, Pallas kernels, exchange(): pl.pallas_call(exchange_kernel, out_shape=[jax.ShapeDtypeStruct((4, 2, 2,...  43.7 us
    pallas_call x1, Pallas kernels, stack(): pl.pallas_call(functools.partial(stack_kernel, count), grid=(HALF // coun...  7.99 us
    unnamed x4, local copies, waits for them, and re-layouts  1.92 us

profile of v2, /device:TPU:1, one launch (start us, length us, event | category | flops | bytes accessed | tf_op | source)
XLA Modules:
  0.0 53.6 jit_solution(12547721220816018858)
XLA Ops:
  0.0 0.0 copy-start
  0.0 1.3 %copy-done = bf16[192,3000]{1,0:T(8,128)(2,1)S(1)} copy-done((bf16[192,3000]{1,0:T(8,128)(2,1)S(1)}, bf16[192,3000]{1,0:T(8,128)(2,1)}, u32[]{:S(2)}) %copy-start) | copy-done | bytes 1152024
  1.3 0.0 copy-start.1
  1.3 0.7 %copy-done.1 = s32[4]{0:T(128)S(1)} copy-done((s32[4]{0:T(128)S(1)}, s32[4]{0:T(128)}, u32[]{:S(2)}) %copy-start.1) | copy-done | bytes 40
  1.9 43.7 %shard_map.37 = (bf16[4,2,2,4,4,3,16,128]{7,6,5,4,3,2,1,0:T(8,128)(2,1)S(1)}, bf16[2,2,48,16,128]{4,3,2,1,0:T(8,128)(2,1)S(1)}) custom-call(s32[4]{0:T(128)S(1)} %copy-done.1, bf16[192,3000]{1,0:T(8,128)(2,1)S(1)} %copy-done, bf16[16,3000,128]{2,1,0:T(8,128)(2,1)} %series_ref.1), custom_call_target="tpu_custom_call" | custom-call | tf_op jit(solution)/shard_map/pallas_call | solution.py:243
  45.6 8.0 %shard_map.38 = bf16[48,1024,128]{2,1,0:T(8,128)(2,1)} custom-call(bf16[4,2,2,48,16,128]{5,4,3,2,1,0:T(8,128)(2,1)S(1)} %bitcast.2, bf16[2,2,48,16,128]{4,3,2,1,0:T(8,128)(2,1)S(1)} %get-tuple-element.8.rhs_ref), custom_call_target="tpu_custom_call" | custom-call | tf_op jit(solution)/shard_map/pallas_call | solution.py:290
Async XLA Ops:
  0.0 1.3 %copy-start = (bf16[192,3000]{1,0:T(8,128)(2,1)S(1)}, bf16[192,3000]{1,0:T(8,128)(2,1)}, u32[]{:S(2)}) copy-start(bf16[192,3000]{1,0:T(8,128)(2,1)} %constant.2.clone.table_ref) | copy-start | bytes 3456004
  1.3 0.7 %copy-start.1 = (s32[4]{0:T(128)S(1)}, s32[4]{0:T(128)}, u32[]{:S(2)}) copy-start(s32[4]{0:T(128)} %ids_ref.1) | copy-start | bytes 52

commit v3 on v2

--- a/solution.py
+++ b/solution.py
@@ -30,11 +30,25 @@
     return jnp.asarray(rows * hann[None, :], jnp.bfloat16)
 
 
+def product(left, right, pair):
+    tiles = [tile.astype(jnp.float32) * (1.0 / WINDOWS) for tile in right]
+    turned = [t for tile in tiles for t in (tile[PART:], -tile[:PART])]
+    factor = jnp.concatenate(
+        [jnp.concatenate(tiles, axis=0), jnp.concatenate(turned, axis=0)], axis=1
+    ).astype(jnp.bfloat16)
+    total = lax.dot_general(
+        jnp.concatenate(left, axis=1), factor, COL, preferred_element_type=jnp.float32
+    )
+    pair[pl.ds(0, 256, 2), :] = total[:, :128]
+    pair[pl.ds(1, 256, 2), :] = total[:, 128:]
+    return pair[...].astype(jnp.bfloat16)
+
+
 def exchange_kernel(
-    ids_ref, table_ref, series_ref, src_ref, rhs_ref,
-    held, rows, v, p1_0, p1_1, q1, p2_0, p2_1, q2, p3, q3,
-    s_sem, l_sem, w_send, w_recv, a1_send, a1_recv, a2_send, a2_recv, y_send, y_recv,
-    b1_send, b1_recv, b2_send, b2_recv, c_send, c_recv,
+    ids_ref, table_ref, series_ref, done_ref, late_ref, rhs_out,
+    held, rows, v, rhs_ref, src_ref, lines, pairs, p1_0, p1_1, q1, p2_0, p2_1, q2, p3, q3,
+    s_sem, o_sem, l_sem, w_send, w_recv, a1_send, a1_recv, a2_send, a2_recv, y_send, y_recv,
+    b1_send, b1_recv, b2_send, b2_recv, h_send, h_recv, c_send, c_recv,
 ):
     me = lax.axis_index("chan")
     w = lax.axis_index("win")
@@ -177,19 +191,18 @@
         k, m = (4 - k) % 4, (4 - m) % 4
         return ((a + k) % 4, (b + m) % 4) if s == 0 else ((a + m) % 4, (b + k) % 4)
 
-    def piece(s, k, m):
+    def piece(s, k, m, only=None):
+        which = slots[s] if only is None else pl.ds(2 * s + only, 1)
         pa, pb = at(s, k, m)
-        return src_ref.at[slots[s], :, c, pa, pb]
-
-    def line(s, m):
-        pa, pb = at(s, 0, m)
-        if s == 0:
-            return src_ref.at[slots[s], :, c, :, pb]
-        return src_ref.at[slots[s], :, c, pa]
-
+        if m < 2:
+            return src_ref.at[which, :, c, pa, pb]
+        return late_ref.at[m - 2, which, :, c, pb if s else pa]
+
+    sibling = (chan(z, x, y, 1 - c), w)
+    beside = (chan(z, x, 1 - y, c), w)
     keep = pltpu.make_async_copy(q3, src_ref.at[:, :, c, a, b], l_sem.at[1])
     keep.start()
-    fourth, fifth, last = {}, {}, []
+    fourth, fifth, across, last = {}, {}, {}, {}
     for k in (1, 3, 2):
         for s in range(2):
             to = at(s, 4 - k, 0)
@@ -199,35 +212,95 @@
             )
             fourth[s, k].start()
 
-    def forward(s, k):
-        for m in (1, 3, 2):
-            to = at(s, 0, 4 - m)
-            fifth[s, k, m] = remote(
-                q3.at[slots[s]] if k == 0 else piece(s, k, 0), piece(s, k, 0),
-                b2_send.at[s, k, m], b2_recv.at[s, k, m], (plane(w, to[0], to[1], c), w),
-            )
-            fifth[s, k, m].start()
-
+    def forward(s, k, m):
+        to = at(s, 0, 4 - m)
+        only = y if m == 2 else None
+        src = piece(s, k, 0, only)
+        if k == 0:
+            src = q3.at[slots[s] if only is None else pl.ds(2 * s + y, 1)]
+        pa, pb = at(s, k, 0)
+        dst = piece(s, k, 0)
+        if m >= 2:
+            which = slots[s] if only is None else pl.ds(2 * s + only, 1)
+            dst = late_ref.at[m - 2, which, :, c, pb if s else pa]
+        fifth[s, k, m] = remote(
+            src, dst, b2_send.at[s, k, m], b2_recv.at[s, k, m], (plane(w, to[0], to[1], c), w)
+        )
+        fifth[s, k, m].start()
+
+    def share(s, k, m):
+        src = q3.at[slots[s]] if k == m == 0 else piece(s, k, m)
+        last[s, k, m] = remote(
+            src, piece(s, k, m), c_send.at[s, k, m], c_recv.at[s, k, m], sibling
+        )
+        last[s, k, m].start()
+
+    def products(s, m):
+        for k in range(4):
+            last[s, k, m].wait()
+
+        def some(n, carry):
+            pa, pb = at(s, 0, m)
+            pa, pb = (pa, n) if s else (n, pb)
+            for e in range(3):
+                f = pa * 12 + pb * 3 + e
+                left = [src_ref[2 * s + j, :, :, pa, pb, e].reshape(8 * PART, 128) for j in range(2)]
+                right = [rhs_ref[g, part, f] for g in range(2) for part in range(2)]
+                lines[m, s, n, e] = product(left, right, pairs.at[e])
+            return carry
+
+        for n in range(4):
+            some(n, 0)
+        out = pltpu.make_async_copy(lines.at[m, s], done_ref.at[m, s], o_sem.at[m, s])
+        out.start()
+        outs.append(out)
+
+    outs = []
+    for m in (2, 1, 3):
+        for s in range(2):
+            forward(s, 0, m)
     for s in range(2):
-        forward(s, 0)
+        share(s, 0, 0)
     keep.wait()
     for k in (1, 3, 2):
         for s in range(2):
             fourth[s, k].wait()
-            forward(s, k)
-    sibling = (chan(z, x, y, 1 - c), w)
-    for m in (0, 1, 3, 2):
-        for s in range(2):
-            if m:
-                for k in range(4):
-                    fifth[s, k, m].wait()
-            last.append(remote(line(s, m), line(s, m), c_send.at[s, m], c_recv.at[s, m], sibling))
-            last[-1].start()
-    for copy in last:
-        copy.wait()
+            for m in (2, 1, 3):
+                forward(s, k, m)
+            share(s, k, 0)
     for copy in windows:
         copy.wait()
     own_rhs.wait()
+    hand = pltpu.make_async_copy(rhs_ref, rhs_out, l_sem.at[0])
+    hand.start()
+    for s in range(2):
+        products(s, 0)
+    order = (0, 1, 3, 2)
+    for k in order:
+        for s in range(2):
+            fifth[s, k, 2].wait()
+            across[s, k] = remote(
+                piece(s, k, 2, y), piece(s, k, 2, y), h_send.at[s, k], h_recv.at[s, k], beside
+            )
+            across[s, k].start()
+    for m in (1, 3):
+        for k in order:
+            for s in range(2):
+                fifth[s, k, m].wait()
+                share(s, k, m)
+    for s in range(2):
+        products(s, 1)
+    for k in order:
+        for s in range(2):
+            across[s, k].wait()
+            share(s, k, 2)
+    for m in (2, 3):
+        for k in range(4):
+            for s in range(2):
+                last[s, k, m].wait()
+    for copy in outs:
+        copy.wait()
+    hand.wait()
     for copy in first:
         copy.wait_send()
     for h in range(2):
@@ -243,7 +316,8 @@
     return pl.pallas_call(
         exchange_kernel,
         out_shape=[
-            jax.ShapeDtypeStruct((4, 2, 2, 4, 4, 3, 2 * PART, 128), jnp.bfloat16),
+            jax.ShapeDtypeStruct((2, 2, 4, 3, 512, 128), jnp.bfloat16),
+            jax.ShapeDtypeStruct((2, 4, 2, 2, 4, 3, 2 * PART, 128), jnp.bfloat16),
             jax.ShapeDtypeStruct((2, 2, HALF, 2 * PART, 128), jnp.bfloat16),
         ],
         in_specs=[
@@ -251,60 +325,93 @@
             pl.BlockSpec(memory_space=pltpu.VMEM),
             pl.BlockSpec(memory_space=pl.ANY),
         ],
-        out_specs=[pl.BlockSpec(memory_space=pl.ANY), pl.BlockSpec(memory_space=pl.ANY)],
+        out_specs=[pl.BlockSpec(memory_space=pl.ANY)] * 3,
         scratch_shapes=[
             pltpu.VMEM((WINS, LENGTH, 128), jnp.bfloat16),
             pltpu.VMEM((2 * NFREQ * PART, 128), jnp.float32),
-            vmem(2, NFREQ), vmem(4, 2, 12), vmem(4, 2, 12), vmem(2, 4, 12), vmem(4, 4, 3), vmem(4, 4, 3),
+            vmem(2, NFREQ), vmem(2, 2, HALF), vmem(4, 2, 2, 4, 4, 3),
+            pltpu.VMEM((2, 2, 4, 3, 512, 128), jnp.bfloat16),
+            pltpu.VMEM((3, 512, 128), jnp.float32),
+            vmem(4, 2, 12), vmem(4, 2, 12), vmem(2, 4, 12), vmem(4, 4, 3), vmem(4, 4, 3),
             vmem(2, 4, 3),
             vmem(2, 2, 4, 3), vmem(4, 2, 3),
-            dma((WINS // GROUP,)), dma((2,)), dma((2,)), dma((2,)),
+            dma((WINS // GROUP,)), dma((2, 2)), dma((2,)), dma((2,)), dma((2,)),
             dma((2, 2, 4)), dma((2, 4, 2)), dma((2, 4)), dma((2, 4)), dma((3,)), dma((3,)),
             dma((2, 4)), dma((2, 4)), dma((2, 4, 4)), dma((2, 4, 4)), dma((2, 4)), dma((2, 4)),
+            dma((2, 4, 4)), dma((2, 4, 4)),
         ],
         compiler_params=pltpu.CompilerParams(
-            collective_id=0, has_side_effects=True, vmem_limit_bytes=46 * 2**20
+            collective_id=0, has_side_effects=True, vmem_limit_bytes=42 * 2**20
         ),
     )(block_ids, make_table(), series)
 
 
-def stack_kernel(count, src_ref, rhs_ref, out_ref, rows_ref):
-    for i in range(count):
-        left = jnp.concatenate(
-            [src_ref[j, :, :, i].reshape(8 * PART, 128) for j in range(4)], axis=1
-        )
-        tiles = [rhs_ref[g, part, i].astype(jnp.float32) * (1.0 / WINDOWS)
-                 for g in range(2) for part in range(2)]
-        turned = [t for tile in tiles for t in (tile[PART:], -tile[:PART])]
-        right = jnp.concatenate(
-            [jnp.concatenate(tiles, axis=0), jnp.concatenate(turned, axis=0)], axis=1
-        ).astype(jnp.bfloat16)
-        total = lax.dot_general(left, right, COL, preferred_element_type=jnp.float32)
-        rows_ref[i % 2, pl.ds(0, 512, 2), :] = total[:, :128]
-        rows_ref[i % 2, pl.ds(1, 512, 2), :] = total[:, 128:]
-        out_ref[i] = rows_ref[i % 2].astype(jnp.bfloat16)
-
-
-def stack(sources, rhs):
-    count = 8
+def stack_kernel(done_ref, late_ref, rhs_ref, out_ref, ready, pairs, d_sem, o_sem):
+    me = lax.axis_index("chan")
+    w = lax.axis_index("win")
+    z, x = me // 16, me // 4 % 4
+    a = jnp.where(w == 0, z, x)
+    b = jnp.where(w == 0, x, z)
+
+    def line(s, m):
+        if s == 0:
+            return out_ref.at[:, (b - m + 4) % 4, :, 0]
+        return out_ref.at[(a - m + 4) % 4, :, :, 1]
+
+    copies = []
+    for m in range(2):
+        for s in range(2):
+            copies.append(
+                pltpu.make_async_copy(done_ref.at[m, s], line(s, m), d_sem.at[m, s])
+            )
+            copies[-1].start()
+    for m in (3, 2):
+        for s in range(2):
+            for n in range(4):
+                pa, pb = (a - m + 4) % 4, (b - m + 4) % 4
+                pa, pb = (pa, n) if s else (n, pb)
+                for e in range(3):
+                    f = pa * 12 + pb * 3 + e
+                    left = [
+                        late_ref[m - 2, 2 * s + j, :, :, n, e].reshape(8 * PART, 128)
+                        for j in range(2)
+                    ]
+                    right = [rhs_ref[g, part, f] for g in range(2) for part in range(2)]
+                    ready[m - 2, s, n, e] = product(left, right, pairs.at[n % 2 * 3 + e])
+                copies.append(
+                    pltpu.make_async_copy(
+                        ready.at[m - 2, s, n], out_ref.at[pa, pb, :, s], o_sem.at[m - 2, s, n]
+                    )
+                )
+                copies[-1].start()
+    for copy in copies:
+        copy.wait()
+
+
+def stack(done, late, rhs):
+    dma = pltpu.SemaphoreType.DMA
     out = pl.pallas_call(
-        functools.partial(stack_kernel, count),
-        grid=(HALF // count,),
+        stack_kernel,
         in_specs=[
-            pl.BlockSpec((4, 2, 2, count, 2 * PART, 128), lambda i: (0, 0, 0, i, 0, 0)),
-            pl.BlockSpec((2, 2, count, 2 * PART, 128), lambda i: (0, 0, i, 0, 0)),
+            pl.BlockSpec(memory_space=pl.ANY),
+            pl.BlockSpec(memory_space=pltpu.VMEM),
+            pl.BlockSpec(memory_space=pltpu.VMEM),
         ],
-        out_specs=pl.BlockSpec((count, 1024, 128), lambda i: (i, 0, 0)),
-        out_shape=jax.ShapeDtypeStruct((HALF, 1024, 128), jnp.bfloat16),
-        scratch_shapes=[pltpu.VMEM((2, 1024, 128), jnp.float32)],
-        compiler_params=pltpu.CompilerParams(vmem_limit_bytes=40 * 2**20),
-    )(sources.reshape(4, 2, 2, HALF, 2 * PART, 128), rhs)
+        out_specs=pl.BlockSpec(memory_space=pl.ANY),
+        out_shape=jax.ShapeDtypeStruct((4, 4, 3, 2, 512, 128), jnp.bfloat16),
+        scratch_shapes=[
+            pltpu.VMEM((2, 2, 4, 3, 512, 128), jnp.bfloat16),
+            pltpu.VMEM((6, 512, 128), jnp.float32),
+            dma((2, 2)),
+            dma((2, 2, 4)),
+        ],
+        compiler_params=pltpu.CompilerParams(vmem_limit_bytes=32 * 2**20),
+    )(done, late, rhs)
     return out.reshape(HALF, 512, 2, 128)
 
 
 def local(series, block_ids):
-    sources, rhs = exchange(block_ids, series)
-    return stack(sources, rhs)
+    return stack(*exchange(block_ids, series))
 
 
 def solution(mesh):

time: 53.8 us -> 51.8 us (0.963)
  Pallas kernels: 51.7 us -> 49.6 us
    pallas_call x2, Pallas kernels: 51.7 us -> 49.6 us  [the longest x1 44.8 us: exchange(): pl.pallas_call(exchange_kernel, out_shape=[jax.ShapeDtypeStruct((2, 2, 4,...]
where the time goes in v3:
time: 51.8 us; the launch traced here: 51.7 us
  Pallas kernels  49.6 us (96%)
  local copies, waits for them, and re-layouts  1.92 us (4%)
    pallas_call x1, Pallas kernels, exchange(): pl.pallas_call(exchange_kernel, out_shape=[jax.ShapeDtypeStruct((2, 2, 4,...  44.8 us
    pallas_call x1, Pallas kernels, stack(): pl.pallas_call(stack_kernel, in_specs=[pl.BlockSpec(memory_space=pl.ANY),...  4.75 us
    unnamed x4, local copies, waits for them, and re-layouts  1.92 us

profile of v3, /device:TPU:1, one launch (start us, length us, event | category | flops | bytes accessed | tf_op | source)
XLA Modules:
  0.0 51.7 jit_solution(6984050480859348705)
XLA Ops:
  0.0 0.0 copy-start
  0.0 1.3 %copy-done = bf16[192,3000]{1,0:T(8,128)(2,1)S(1)} copy-done((bf16[192,3000]{1,0:T(8,128)(2,1)S(1)}, bf16[192,3000]{1,0:T(8,128)(2,1)}, u32[]{:S(2)}) %copy-start) | copy-done | bytes 1152024
  1.3 0.0 copy-start.1
  1.3 0.7 %copy-done.1 = s32[4]{0:T(128)S(1)} copy-done((s32[4]{0:T(128)S(1)}, s32[4]{0:T(128)}, u32[]{:S(2)}) %copy-start.1) | copy-done | bytes 40
  1.9 44.8 %shard_map.37 = (bf16[2,2,4,3,512,128]{5,4,3,2,1,0:T(8,128)(2,1)S(1)}, bf16[2,4,2,2,4,3,16,128]{7,6,5,4,3,2,1,0:T(8,128)(2,1)S(1)}, bf16[2,2,48,16,128]{4,3,2,1,0:T(8,128)(2,1)S(1)}) custom-call(s32[4]{0:T(128)S(1)} %copy-done.1, bf16[192,3000]{1,0:T(8,128)(2,1)S(1)} %copy-done, bf16[16,3000,128]{2,1,0:T(8,128)(2,1)} %series_ref.1), custom_call_target="tpu_custom_call" | custom-call | tf_op jit(solution)/shard_map/pallas_call | solution.py:316
  46.8 4.7 %shard_map.38 = bf16[4,4,3,2,512,128]{5,4,3,2,1,0:T(8,128)(2,1)} custom-call(bf16[2,2,4,3,512,128]{5,4,3,2,1,0:T(8,128)(2,1)S(1)} %get-tuple-element.8.done_ref, bf16[2,4,2,2,4,3,16,128]{7,6,5,4,3,2,1,0:T(8,128)(2,1)S(1)} %get-tuple-element.9.late_ref, bf16[2,2,48,16,128]{4,3,2,1,0:T(8,128)(2,1)S(1)} %get-tuple-element.10.rhs_ref), custom_call_target="tpu_custom_call" | custom-call | tf_op jit(solution)/shard_map/pallas_call | solution.py:393
Async XLA Ops:
  0.0 1.3 %copy-start = (bf16[192,3000]{1,0:T(8,128)(2,1)S(1)}, bf16[192,3000]{1,0:T(8,128)(2,1)}, u32[]{:S(2)}) copy-start(bf16[192,3000]{1,0:T(8,128)(2,1)} %constant.2.clone.table_ref) | copy-start | bytes 3456004
  1.3 0.7 %copy-start.1 = (s32[4]{0:T(128)S(1)}, s32[4]{0:T(128)}, u32[]{:S(2)}) copy-start(s32[4]{0:T(128)} %ids_ref.1) | copy-start | bytes 52

commit v4 on v3

--- a/solution.py
+++ b/solution.py
@@ -62,7 +62,7 @@
 
     p1 = (p1_0, p1_1)
     p2 = (p2_0, p2_1)
-    column = [(1, 0), (0, 1), (1, 1)]
+    column = [(0, 1), (1, 0), (1, 1)]
     coords = (z, x)
     loads = []
     for n in range(WINS // GROUP):
@@ -90,7 +90,8 @@
         for k in range(GROUP):
             values = held[first + k].astype(jnp.float32)
             level = 2.0 * jnp.sqrt(jnp.mean(values * values, axis=0, keepdims=True) + 1e-6)
-            clipped.append(jnp.clip(values, -level, level).astype(jnp.bfloat16))
+            level = level.astype(jnp.bfloat16)
+            clipped.append(jnp.minimum(jnp.maximum(held[first + k], -level), level))
         spectrum = jnp.dot(
             table_ref[...], jnp.concatenate(clipped, axis=1), preferred_element_type=jnp.float32
         )
@@ -109,7 +110,7 @@
         if part == 0:
             pl.semaphore_wait(barrier, len(peers))
         other = (c + part) % 2
-        for k in (1, 3, 2, 0):
+        for k in (2, 1, 3, 0):
             for h in range(2):
                 a, b = coords[h], coords[1 - h]
                 to_a = (a + k) % 4
@@ -151,7 +152,7 @@
                     ).wait_recv()
         for j in range(4):
             q1[h, j] = p1[h][where[j][h], where[j][3]]
-        for k in (1, 3, 2):
+        for k in (2, 1, 3):
             to_b = (b + k) % 4
             copy = remote(
                 q1.at[h, :, pl.ds(to_b * 3, 3)], p2[h].at[b],
@@ -203,7 +204,7 @@
     keep = pltpu.make_async_copy(q3, src_ref.at[:, :, c, a, b], l_sem.at[1])
     keep.start()
     fourth, fifth, across, last = {}, {}, {}, {}
-    for k in (1, 3, 2):
+    for k in (2, 1, 3):
         for s in range(2):
             to = at(s, 4 - k, 0)
             fourth[s, k] = remote(

time: 51.8 us -> 50.3 us (0.971)
  Pallas kernels: 49.6 us -> 48.1 us
    pallas_call x1, Pallas kernels: 44.8 us -> 43.4 us  [exchange(): pl.pallas_call(exchange_kernel, out_shape=[jax.ShapeDtypeStruct((2, 2, 4,...]
where the time goes in v4:
time: 50.3 us; the launch traced here: 50.2 us
  Pallas kernels  48.1 us (96%)
  local copies, waits for them, and re-layouts  1.92 us (4%)
    pallas_call x1, Pallas kernels, exchange(): pl.pallas_call(exchange_kernel, out_shape=[jax.ShapeDtypeStruct((2, 2, 4,...  43.4 us
    pallas_call x1, Pallas kernels, stack(): pl.pallas_call(stack_kernel, in_specs=[pl.BlockSpec(memory_space=pl.ANY),...  4.75 us
    unnamed x4, local copies, waits for them, and re-layouts  1.92 us

profile of v4, /device:TPU:1, one launch (start us, length us, event | category | flops | bytes accessed | tf_op | source)
XLA Modules:
  0.0 50.2 jit_solution(12532171968845598604)
XLA Ops:
  0.0 0.0 copy-start
  0.0 1.3 %copy-done = bf16[192,3000]{1,0:T(8,128)(2,1)S(1)} copy-done((bf16[192,3000]{1,0:T(8,128)(2,1)S(1)}, bf16[192,3000]{1,0:T(8,128)(2,1)}, u32[]{:S(2)}) %copy-start) | copy-done | bytes 1152024
  1.3 0.0 copy-start.1
  1.3 0.7 %copy-done.1 = s32[4]{0:T(128)S(1)} copy-done((s32[4]{0:T(128)S(1)}, s32[4]{0:T(128)}, u32[]{:S(2)}) %copy-start.1) | copy-done | bytes 40
  1.9 43.4 %shard_map.37 = (bf16[2,2,4,3,512,128]{5,4,3,2,1,0:T(8,128)(2,1)S(1)}, bf16[2,4,2,2,4,3,16,128]{7,6,5,4,3,2,1,0:T(8,128)(2,1)S(1)}, bf16[2,2,48,16,128]{4,3,2,1,0:T(8,128)(2,1)S(1)}) custom-call(s32[4]{0:T(128)S(1)} %copy-done.1, bf16[192,3000]{1,0:T(8,128)(2,1)S(1)} %copy-done, bf16[16,3000,128]{2,1,0:T(8,128)(2,1)} %series_ref.1), custom_call_target="tpu_custom_call" | custom-call | tf_op jit(solution)/shard_map/pallas_call | solution.py:317
  45.3 4.7 %shard_map.38 = bf16[4,4,3,2,512,128]{5,4,3,2,1,0:T(8,128)(2,1)} custom-call(bf16[2,2,4,3,512,128]{5,4,3,2,1,0:T(8,128)(2,1)S(1)} %get-tuple-element.8.done_ref, bf16[2,4,2,2,4,3,16,128]{7,6,5,4,3,2,1,0:T(8,128)(2,1)S(1)} %get-tuple-element.9.late_ref, bf16[2,2,48,16,128]{4,3,2,1,0:T(8,128)(2,1)S(1)} %get-tuple-element.10.rhs_ref), custom_call_target="tpu_custom_call" | custom-call | tf_op jit(solution)/shard_map/pallas_call | solution.py:394
Async XLA Ops:
  0.0 1.3 %copy-start = (bf16[192,3000]{1,0:T(8,128)(2,1)S(1)}, bf16[192,3000]{1,0:T(8,128)(2,1)}, u32[]{:S(2)}) copy-start(bf16[192,3000]{1,0:T(8,128)(2,1)} %constant.2.clone.table_ref) | copy-start | bytes 3456004
  1.3 0.7 %copy-start.1 = (s32[4]{0:T(128)S(1)}, s32[4]{0:T(128)}, u32[]{:S(2)}) copy-start(s32[4]{0:T(128)} %ids_ref.1) | copy-start | bytes 52

commit v5 on v4

--- a/solution.py
+++ b/solution.py
@@ -247,7 +247,7 @@
                 f = pa * 12 + pb * 3 + e
                 left = [src_ref[2 * s + j, :, :, pa, pb, e].reshape(8 * PART, 128) for j in range(2)]
                 right = [rhs_ref[g, part, f] for g in range(2) for part in range(2)]
-                lines[m, s, n, e] = product(left, right, pairs.at[e])
+                lines[m, s, n, e] = product(left, right, pairs.at[n % 2 * 3 + e])
             return carry
 
         for n in range(4):
@@ -332,7 +332,7 @@
             pltpu.VMEM((2 * NFREQ * PART, 128), jnp.float32),
             vmem(2, NFREQ), vmem(2, 2, HALF), vmem(4, 2, 2, 4, 4, 3),
             pltpu.VMEM((2, 2, 4, 3, 512, 128), jnp.bfloat16),
-            pltpu.VMEM((3, 512, 128), jnp.float32),
+            pltpu.VMEM((6, 512, 128), jnp.float32),
             vmem(4, 2, 12), vmem(4, 2, 12), vmem(2, 4, 12), vmem(4, 4, 3), vmem(4, 4, 3),
             vmem(2, 4, 3),
             vmem(2, 2, 4, 3), vmem(4, 2, 3),

time: 50.3 us -> 50.4 us (level)
  no operation moved by 1% of the time
where the time goes in v5:
time: 50.4 us; the launch traced here: 50.2 us
  Pallas kernels  48.1 us (95%)
  local copies, waits for them, and re-layouts  1.92 us (4%)
    pallas_call x1, Pallas kernels, exchange(): pl.pallas_call(exchange_kernel, out_shape=[jax.ShapeDtypeStruct((2, 2, 4,...  43.4 us
    pallas_call x1, Pallas kernels, stack(): pl.pallas_call(stack_kernel, in_specs=[pl.BlockSpec(memory_space=pl.ANY),...  4.75 us
    unnamed x4, local copies, waits for them, and re-layouts  1.92 us

profile of v5, /device:TPU:1, one launch (start us, length us, event | category | flops | bytes accessed | tf_op | source)
XLA Modules:
  0.0 50.2 jit_solution(12997782321343223659)
XLA Ops:
  0.0 0.0 copy-start
  0.0 1.3 %copy-done = bf16[192,3000]{1,0:T(8,128)(2,1)S(1)} copy-done((bf16[192,3000]{1,0:T(8,128)(2,1)S(1)}, bf16[192,3000]{1,0:T(8,128)(2,1)}, u32[]{:S(2)}) %copy-start) | copy-done | bytes 1152024
  1.3 0.0 copy-start.1
  1.3 0.7 %copy-done.1 = s32[4]{0:T(128)S(1)} copy-done((s32[4]{0:T(128)S(1)}, s32[4]{0:T(128)}, u32[]{:S(2)}) %copy-start.1) | copy-done | bytes 40
  1.9 43.4 %shard_map.37 = (bf16[2,2,4,3,512,128]{5,4,3,2,1,0:T(8,128)(2,1)S(1)}, bf16[2,4,2,2,4,3,16,128]{7,6,5,4,3,2,1,0:T(8,128)(2,1)S(1)}, bf16[2,2,48,16,128]{4,3,2,1,0:T(8,128)(2,1)S(1)}) custom-call(s32[4]{0:T(128)S(1)} %copy-done.1, bf16[192,3000]{1,0:T(8,128)(2,1)S(1)} %copy-done, bf16[16,3000,128]{2,1,0:T(8,128)(2,1)} %series_ref.1), custom_call_target="tpu_custom_call" | custom-call | tf_op jit(solution)/shard_map/pallas_call | solution.py:317
  45.3 4.7 %shard_map.38 = bf16[4,4,3,2,512,128]{5,4,3,2,1,0:T(8,128)(2,1)} custom-call(bf16[2,2,4,3,512,128]{5,4,3,2,1,0:T(8,128)(2,1)S(1)} %get-tuple-element.8.done_ref, bf16[2,4,2,2,4,3,16,128]{7,6,5,4,3,2,1,0:T(8,128)(2,1)S(1)} %get-tuple-element.9.late_ref, bf16[2,2,48,16,128]{4,3,2,1,0:T(8,128)(2,1)S(1)} %get-tuple-element.10.rhs_ref), custom_call_target="tpu_custom_call" | custom-call | tf_op jit(solution)/shard_map/pallas_call | solution.py:394
Async XLA Ops:
  0.0 1.3 %copy-start = (bf16[192,3000]{1,0:T(8,128)(2,1)S(1)}, bf16[192,3000]{1,0:T(8,128)(2,1)}, u32[]{:S(2)}) copy-start(bf16[192,3000]{1,0:T(8,128)(2,1)} %constant.2.clone.table_ref) | copy-start | bytes 3456004
  1.3 0.7 %copy-start.1 = (s32[4]{0:T(128)S(1)}, s32[4]{0:T(128)}, u32[]{:S(2)}) copy-start(s32[4]{0:T(128)} %ids_ref.1) | copy-start | bytes 52
